TPU v7x, 32 devices: a whole 2x2x4 slice. The times are simulated.
32 devices in a mesh: ctx: 8 (over z, y), tp: 4 (over x, core).
Axes of the slice: x: 2, y: 2, z: 4, core: 2. Of those that a mesh axis runs over, the one named last changes fastest.
Arguments:
- hidden_in: bfloat16 [4096, 4608], P('ctx'), may hold values from -5.4 to 5.4
- pre_gain: float32 [4608], replicated, may hold values from 0.25 to 1.75
- w_query: bfloat16 [4608, 2048], P(None, 'tp'), may hold values from -0.677644 to 0.677644
- w_key: bfloat16 [4608, 1024], P(None, 'tp'), may hold values from -0.058925565 to 0.058925565
- w_value: bfloat16 [4608, 1024], P(None, 'tp'), may hold values from -0.09375 to 0.09375
- w_out: bfloat16 [2048, 4608], P('tp'), may hold values from -0.26516504 to 0.26516504
- post_gain: float32 [4608], P('tp'), may hold values from 0.25 to 1.75
Outputs:
- layer_out: bfloat16 [4096, 4608], P('ctx', 'tp')
- sink_share: float32 [4096], P('ctx')
All inputs are finite; a program needn't handle non-finite values.
Results may differ from a plain program's by a relative error of at most 0.0095.
The roundings to bfloat16 on the way count: a program that leaves them out, or rounds other values in their place, can miss the bound.
Values may be sent and summed in bfloat16 or wider, within the bound.
A program may use at most 192 MiB of HBM per device.

v0:
```python
import jax
import jax.numpy as jnp
from jax import lax
from jax.sharding import PartitionSpec as P

D = 4608
QHEADS = 16
HEAD = 128
WINDOW = 4096
SINKS = 4


def shifted(x, axis, by):
    devices = lax.axis_size(axis)
    pairs = [(i, i + by) for i in range(devices) if 0 <= i + by < devices]
    return lax.ppermute(x, axis, pairs)


def spread(value, axis, source):
    kept = jnp.where(lax.axis_index(axis) == source, value, 0).astype(value.dtype)
    return lax.psum(kept, axis)


def rope_tables(positions):
    index = jnp.arange(0, HEAD, 2).astype(jnp.float32)
    inverse = jnp.exp(-jnp.log(jnp.float32(10000.0)) * index / HEAD)
    angles = positions.astype(jnp.float32)[:, None] * inverse[None, :]
    angles = jnp.concatenate([angles, angles], axis=1)
    return (jnp.cos(angles)[:, None, :], jnp.sin(angles)[:, None, :])


def rotate(values, cosine_table, sine_table):
    half = values.shape[-1] // 2
    turned = jnp.concatenate([-values[..., half:], values[..., :half]], axis=-1)
    return values * cosine_table + turned * sine_table


def project_keys(states, w_key, w_value, positions):
    count = states.shape[0]
    cosine_table, sine_table = rope_tables(positions)
    keys = jnp.dot(states, w_key, preferred_element_type=jnp.float32).reshape(count, -1, HEAD)
    keys = rotate(keys, cosine_table, sine_table).astype(jnp.bfloat16).reshape(count, -1)
    values = jnp.dot(states, w_value, preferred_element_type=jnp.float32).astype(jnp.bfloat16)
    return (keys, values)


def on_device(hidden_in, pre_gain, w_query, w_key, w_value, w_out, post_gain):
    tok_rows = hidden_in.shape[0]
    local_q = w_query.shape[1] // HEAD
    local_kv = w_key.shape[1] // HEAD
    group = local_q // local_kv
    offset = lax.axis_index("ctx") * tok_rows
    inputs = hidden_in.astype(jnp.float32)
    normed = (
        inputs * lax.rsqrt(jnp.mean(inputs * inputs, axis=-1, keepdims=True) + 1e-06) * pre_gain
    ).astype(jnp.bfloat16)
    positions = offset + jnp.arange(tok_rows, dtype=jnp.int32)
    cosine_table, sine_table = rope_tables(positions)
    query = jnp.dot(normed, w_query, preferred_element_type=jnp.float32).reshape(
        tok_rows, local_q, HEAD
    )
    query = (
        rotate(query, cosine_table, sine_table)
        .astype(jnp.bfloat16)
        .reshape(tok_rows, local_kv, group, HEAD)
    )
    keys, values = project_keys(normed, w_key, w_value, positions)
    reach = WINDOW // tok_rows
    pieces = []
    for distance in range(reach, 0, -1):
        pieces.append(shifted((keys, values), "ctx", distance))
    keys_all = jnp.concatenate([piece[0] for piece in pieces] + [keys], axis=0)
    values_all = jnp.concatenate([piece[1] for piece in pieces] + [values], axis=0)
    sink_keys, sink_values = (spread(keys[:SINKS], "ctx", 0), spread(values[:SINKS], "ctx", 0))
    sink_keys = sink_keys.reshape(SINKS, local_kv, HEAD)
    sink_values = sink_values.reshape(SINKS, local_kv, HEAD)
    block_rows = min(512, tok_rows)
    span = WINDOW + block_rows

    def one_block(block_index):
        start = block_index * block_rows
        key_block = keys_all.reshape(span, local_kv, HEAD)
        value_block = values_all.reshape(span, local_kv, HEAD)
        scores = (
            jnp.einsum("qkgd,lkd->kgql", query, key_block, preferred_element_type=jnp.float32)
            / 12.0
        )
        scores = 50.0 * jnp.tanh(scores / 50.0)
        sink_scores = (
            jnp.einsum("qkgd,lkd->kgql", query, sink_keys, preferred_element_type=jnp.float32)
            / 12.0
        )
        sink_scores = 50.0 * jnp.tanh(sink_scores / 50.0)
        query_pos = offset + start + jnp.arange(block_rows, dtype=jnp.int32)
        key_pos = offset + start - WINDOW + jnp.arange(span, dtype=jnp.int32)
        distance_map = query_pos[:, None] - key_pos[None, :]
        live = (key_pos[None, :] >= SINKS) & (distance_map >= 0) & (distance_map < WINDOW)
        sink_live = query_pos[:, None] - jnp.arange(SINKS, dtype=jnp.int32)[None, :] >= 0
        expo = jnp.where(live, jnp.exp(scores), 0.0)
        sink_expo = jnp.where(sink_live, jnp.exp(sink_scores), 0.0)
        total = jnp.sum(expo, axis=-1) + jnp.sum(sink_expo, axis=-1)
        weight = expo / total[..., None]
        sink_weight = sink_expo / total[..., None]
        sink_sum = jnp.sum(sink_expo, axis=-1)
        attended = jnp.einsum(
            "kgql,lkd->qkgd",
            weight.astype(jnp.bfloat16),
            value_block,
            preferred_element_type=jnp.float32,
        )
        attended = attended + jnp.einsum(
            "kgql,lkd->qkgd",
            sink_weight.astype(jnp.bfloat16),
            sink_values,
            preferred_element_type=jnp.float32,
        )
        attended = attended.astype(jnp.bfloat16).reshape(block_rows, local_q * HEAD)
        return (attended, jnp.sum(sink_sum, axis=(0, 1)))

    attended, sink_sums = lax.map(one_block, jnp.arange(tok_rows // block_rows, dtype=jnp.int32))
    attended = attended.reshape(tok_rows, local_q * HEAD)
    sink_sums = sink_sums.reshape(tok_rows)
    cols_dev = post_gain.shape[0]
    partial_rows = jnp.dot(attended, w_out, preferred_element_type=jnp.float32)
    projected = lax.psum_scatter(partial_rows, "tp", scatter_dimension=1, tiled=True)
    squares = jnp.sum(projected * projected, axis=-1)
    total_squares, total_sinks = lax.psum((squares, sink_sums), "tp")
    post = projected * lax.rsqrt(total_squares / D + 1e-06)[:, None] * post_gain
    own_cols = lax.dynamic_slice_in_dim(inputs, lax.axis_index("tp") * cols_dev, cols_dev, 1)
    layer_out = (own_cols + post).astype(jnp.bfloat16)
    sink_share = jnp.log(total_sinks / QHEADS)
    return (layer_out, sink_share)


def solution(mesh):
    return jax.shard_map(
        on_device,
        mesh=mesh,
        in_specs=(
            P("ctx", None),
            P(),
            P(None, "tp"),
            P(None, "tp"),
            P(None, "tp"),
            P("tp", None),
            P("tp"),
        ),
        out_specs=(P("ctx", "tp"), P("ctx")),
        check_vma=False,
    )
```

profile of v0, /device:TPU:25, one launch (start us, length us, event | category | flops | bytes accessed | tf_op | source)
XLA Modules:
  0.0 310.6 jit_solution(4353033533650330806)
XLA Ops:
  8.6 3.6 %multiply_reduce_fusion = f32[512]{0:T(512)S(1)} fusion(bf16[512,4608]{1,0:T(8,128)(2,1)} %param.7), kind=kLoop, calls=%fused_computation.7 | loop fusion | flops 7077376 | bytes 4720640 | tf_op jit(solution)/shard_map/reduce_sum | solution.py:55
  12.6 1.8 fusion.30
  16.2 1.5 collective-permute-start.8
  17.7 1.4 collective-permute-start.9
  19.1 1.3 collective-permute-start.10
  20.4 1.3 collective-permute-start.11
  21.7 5.2 %convolution_convert_fusion = bf16[512,256]{1,0:T(8,128)(2,1)} fusion(bf16[4608,256]{1,0:T(8,128)(2,1)} %param.11, f32[4608]{0:T(1024)S(1)} %copy-done.14, f32[512]{0:T(512)S(1)} %add_rsqrt_fusion.1, bf16[512,4608]{1,0:T(8,128)(2,1)} %param.7), kind=kOutput, calls=%fused_computation.16 | convolution fusion | flops 1217527808 | bytes 7360512 | tf_op jit(solution)/shard_map/dot_general | solution.py:43
  26.9 1.4 collective-permute-start
  29.0 6.9 %fusion.29 = f32[512,512]{0,1:T(8,128)S(1)} fusion(bf16[4608,512]{1,0:T(8,128)(2,1)} %param.9, f32[4608]{0:T(1024)S(1)} %copy-done.15, f32[512]{0:T(512)} %copy-done.13, bf16[512,4608]{1,0:T(8,128)(2,1)} %param.7), kind=kOutput, calls=%fused_computation.75 | convolution fusion | flops 2425356288 | bytes 10506240 | tf_op jit(solution)/shard_map/dot_general | solution.py:59
  37.1 1.4 copy.24
  38.5 1.3 copy.22
  39.9 1.6 fusion.14
  41.6 4.7 %fusion.3 = pred[512,4608]{0,1:T(8,128)(4,1)} fusion(s32[4608]{0:T(1024)S(1)} %copy-done.11, s32[512]{0:T(512)S(1)} %iota_add_fusion.1, pred[4608]{0:T(1024)(128)(4,1)S(1)} %broadcast_compare_fusion), kind=kLoop, calls=%fused_computation.9 | loop fusion | flops 11796480 | bytes 2384384 | tf_op jit(solution)/shard_map/while/body/eval_jaxpr/and | solution.py:97
  47.7 17.3 %all-reduce.1 = (bf16[4,2,128]{2,0,1:T(4,128)(2,1)S(1)}, bf16[4,2,128]{2,0,1:T(4,128)(2,1)S(1)}) all-reduce(bf16[4,2,128]{2,0,1:T(4,128)(2,1)S(1)} %fusion.21, bf16[4,2,128]{2,0,1:T(4,128)(2,1)S(1)} %fusion.22), channel_id=1, replica_groups=mesh['ctx'=8,'tp'=4] {'ctx'}, use_global_device_ids=true, to_apply=%region_2.3 | all-reduce | flops 2048 | bytes 8192 | tf_op jit(solution)/shard_map/psum | solution.py:21
  67.1 1.1 copy.13
  68.2 1.3 collective-permute-start.12
  69.5 1.3 collective-permute-start.13
  70.8 1.3 collective-permute-start.2
  72.8 1.3 collective-permute-start.3
  75.1 1.3 collective-permute-start.4
  76.4 14.0 %collective-permute-done.12 = bf16[512,256]{0,1:T(8,128)(2,1)S(1)} collective-permute-done((bf16[512,256]{0,1:T(8,128)(2,1)}, bf16[512,256]{0,1:T(8,128)(2,1)S(1)}, u32[]{:S(2)}, u32[]{:S(2)}) %collective-permute-start.12) | collective-permute-done | bytes 262176 | tf_op jit(solution)/shard_map/ppermute | solution.py:16
  90.5 1.3 collective-permute-start.14
  91.8 22.8 %collective-permute-done.13 = bf16[512,256]{0,1:T(8,128)(2,1)S(1)} collective-permute-done((bf16[512,256]{0,1:T(8,128)(2,1)}, bf16[512,256]{0,1:T(8,128)(2,1)S(1)}, u32[]{:S(2)}, u32[]{:S(2)}) %collective-permute-start.13) | collective-permute-done | bytes 262176 | tf_op jit(solution)/shard_map/ppermute | solution.py:16
  114.6 1.9 collective-permute-start.15
  116.5 1.3 collective-permute-start.5
  117.8 1.3 collective-permute-start.6
  119.1 3.6 %collective-permute-done.4 = bf16[512,256]{1,0:T(8,128)(2,1)S(1)} collective-permute-done((bf16[512,256]{1,0:T(8,128)(2,1)}, bf16[512,256]{1,0:T(8,128)(2,1)S(1)}, u32[]{:S(2)}, u32[]{:S(2)}) %collective-permute-start.4) | collective-permute-done | bytes 262176 | tf_op jit(solution)/shard_map/ppermute | solution.py:16
  122.7 2.1 collective-permute-start.7
  124.9 1.8 copy.14
  126.7 1.8 copy.15
  129.7 1.1 copy.18
  130.9 1.8 copy.19
  132.7 1.8 copy.20
  134.5 8.3 %collective-permute-done.5 = bf16[512,256]{1,0:T(8,128)(2,1)} collective-permute-done((bf16[512,256]{1,0:T(8,128)(2,1)}, bf16[512,256]{1,0:T(8,128)(2,1)}, u32[]{:S(2)}, u32[]{:S(2)}) %collective-permute-start.5) | collective-permute-done | bytes 262176 | tf_op jit(solution)/shard_map/ppermute | solution.py:16
  144.8 3.6 %collective-permute-done.7 = bf16[512,256]{1,0:T(8,128)(2,1)} collective-permute-done((bf16[512,256]{1,0:T(8,128)(2,1)}, bf16[512,256]{1,0:T(8,128)(2,1)}, u32[]{:S(2)}, u32[]{:S(2)}) %collective-permute-start.7) | collective-permute-done | bytes 262176 | tf_op jit(solution)/shard_map/ppermute | solution.py:16
  150.3 2.5 copy.34
  152.8 1.8 constant_dynamic-update-slice_fusion.16
  154.6 1.7 constant_dynamic-update-slice_fusion.15
  158.5 1.7 constant_dynamic-update-slice_fusion.11
  160.2 1.7 constant_dynamic-update-slice_fusion.10
  162.6 17.2 %fusion = (f32[2,2,512]{2,1,0:T(2,128)S(1)}, f32[2,4608,512,2]{2,1,3,0:T(8,128)}) fusion(pred[512,4608]{0,1:T(8,128)(4,1)S(1)} %copy-done.6, bf16[512,2,2,128]{3,0,2,1:T(8,128)(2,1)S(1)} %copy-done.9, bf16[4608,2,128]{2,0,1:T(8,128)(2,1)} %constant_dynamic-update-slice_fusion.9), kind=kOutput, calls=%fused_computation.2 | convolution fusion | flops 2453665792 | bytes 42999808 | tf_op jit(solution)/shard_map/while/body/eval_jaxpr/qkgd,lkd->kgql/dot_general | solution.py:85
  180.2 19.5 %fusion.7 = bf16[2,128,2,512]{3,1,2,0:T(8,128)(2,1)} fusion(f32[2,128,2,512]{3,1,2,0:T(8,128)S(1)} %fusion.18, bf16[4608,2,128,1]{0,2,3,1:T(8,128)(2,1)} %bitcast.80, f32[2,4608,512,2]{2,1,3,0:T(8,128)} %get-tuple-element.42, f32[2,2,512]{2,1,0:T(2,128)S(1)} %add.103, pred[512,4608]{0,1:T(8,128)(4,1)S(1)} %copy-done.6), kind=kOutput, calls=%fused_computation.15 | convolution fusion | flops 2463629312 | bytes 44048384 | tf_op jit(solution)/shard_map/while/body/eval_jaxpr/kgql,lkd->qkgd/dot_general | solution.py:105
  199.6 8.8 %fusion.33 = f32[512,4608]{1,0:T(8,128)} fusion(bf16[512,512]{0,1:T(8,128)(2,1)} %bitcast.81, bf16[512,4608]{1,0:T(8,128)(2,1)} %param.12), kind=kOutput, calls=%fused_computation.79 | convolution fusion | flops 2415919104 | bytes 14680064 | tf_op jit(solution)/shard_map/dot_general | solution.py:124
  208.4 7.2 %convert_element_type.56 = f32[512,4608]{1,0:T(8,128)} convert(bf16[512,4608]{1,0:T(8,128)(2,1)} %param.7) | non-fusion elementwise | flops 2359296 | bytes 14155776 | tf_op jit(solution)/shard_map/convert_element_type | solution.py:53
  215.7 76.0 %reduce-scatter.2.cloned.1.call-done = f32[512,1152]{1,0:T(8,128)} async-done(((f32[512,4608]{1,0:T(8,128)}), f32[512,1152]{1,0:T(8,128)}) %reduce-scatter.2.cloned.1.call-update) | async-done | bytes 2359312 | tf_op jit(solution)/shard_map/reduce_scatter | solution.py:125
  291.7 1.9 multiply_reduce_fusion.1
  293.6 5.7 %all-reduce = (f32[512]{0:T(512)S(1)}, f32[512]{0:T(512)S(1)}) all-reduce(f32[512]{0:T(512)S(1)} %multiply_reduce_fusion.1, f32[512]{0:T(512)S(1)} %get-tuple-element.20), channel_id=1, replica_groups=mesh['ctx'=8,'tp'=4] {'tp'}, use_global_device_ids=true, to_apply=%region_7.8 | all-reduce | flops 1024 | bytes 8192 | tf_op jit(solution)/shard_map/psum | solution.py:127
  299.9 3.9 %add_convert_fusion = bf16[512,1152]{1,0:T(8,128)(2,1)} fusion(f32[512,1152]{1,0:T(8,128)} %reduce-scatter.2.cloned.1.call-done, f32[512,4608]{1,0:T(8,128)} %convert_element_type.56, s32[]{:T(128)S(6)} %select_n.30, f32[1152]{0:T(1024)S(1)} %copy-done.12, f32[512]{0:T(512)S(1)} %get-tuple-element.45), kind=kLoop, calls=%fused_computation.12 | loop fusion | flops 2359296 | bytes 5904900 | tf_op jit(solution)/shard_map/convert_element_type | solution.py:130
  (91 shorter events, 19.8 us)
Async XLA Ops:
  7.2 5.0 %copy-start = (bf16[4608,256]{1,0:T(8,128)(2,1)S(1)}, bf16[4608,256]{1,0:T(8,128)(2,1)}, u32[]{:S(2)}) copy-start(bf16[4608,256]{1,0:T(8,128)(2,1)} %param.10) | copy-start | bytes 7077892
  7.2 284.5 %reduce-scatter.2.cloned.1.call-start = ((), (), s32[]{:S(2)}) async-start(), calls=%async_computation.1 | async-start | bytes 11796480 | tf_op jit(solution)/shard_map/reduce_scatter | solution.py:125
  7.4 4.7 %copy-start.14 = (f32[4608]{0:T(1024)S(1)}, f32[4608]{0:T(1024)}, u32[]{:S(2)}) copy-start(f32[4608]{0:T(1024)} %param.8) | copy-start | bytes 55300
  8.5 6.3 %copy-start.5 = (f32[512,128]{1,0:T(8,128)}, f32[512,128]{1,0:T(8,128)S(1)}, u32[]{:S(2)}) copy-start(f32[512,128]{1,0:T(8,128)S(1)} %get-tuple-element.40) | copy-start | bytes 786436
  8.5 20.4 %copy-start.3 = (f32[512,128]{1,0:T(8,128)}, f32[512,128]{1,0:T(8,128)S(1)}, u32[]{:S(2)}) copy-start(f32[512,128]{1,0:T(8,128)S(1)} %get-tuple-element.39) | copy-start | bytes 786436
  8.6 4.0 %copy-start.2 = (bf16[512,4608]{1,0:T(8,128)(2,1)S(1)}, bf16[512,4608]{1,0:T(8,128)(2,1)}, u32[]{:S(2)}) copy-start(bf16[512,4608]{1,0:T(8,128)(2,1)} %param.7) | copy-start | bytes 14155780
  12.6 9.1 %copy-start.13 = (f32[512]{0:T(512)}, f32[512]{0:T(512)S(1)}, u32[]{:S(2)}) copy-start(f32[512]{0:T(512)S(1)} %add_rsqrt_fusion.1) | copy-start | bytes 6148
  15.1 11.9 %copy-start.7 = (f32[512,2,128]{2,0,1:T(8,128)}, f32[512,2,128]{2,0,1:T(8,128)S(1)}, u32[]{:S(2)}) copy-start(f32[512,2,128]{2,0,1:T(8,128)S(1)} %maximum_multiply_fusion.1) | copy-start | bytes 1572868
  16.2 12.7 %copy-start.15 = (f32[4608]{0:T(1024)S(1)}, f32[4608]{0:T(1024)}, u32[]{:S(2)}) copy-start(f32[4608]{0:T(1024)} %param.8) | copy-start | bytes 55300
  16.2 48.7 %collective-permute-start.8 = (bf16[512,256]{0,1:T(8,128)(2,1)}, bf16[512,256]{0,1:T(8,128)(2,1)}, u32[]{:S(2)}, u32[]{:S(2)}) collective-permute-start(bf16[512,256]{0,1:T(8,128)(2,1)} %fusion.15), channel_id=1, source_target_pairs={} | collective-permute-start | bytes 786440 | tf_op jit(solution)/shard_map/ppermute | solution.py:16
  17.7 50.4 %collective-permute-start.9 = (bf16[512,256]{0,1:T(8,128)(2,1)}, bf16[512,256]{0,1:T(8,128)(2,1)}, u32[]{:S(2)}, u32[]{:S(2)}) collective-permute-start(bf16[512,256]{0,1:T(8,128)(2,1)} %fusion.15), channel_id=1, source_target_pairs={{0,28},{1,29},{2,30},{3,31}} | collective-permute-start | bytes 786440 | tf_op jit(solution)/shard_map/ppermute | solution.py:16
  19.1 50.4 %collective-permute-start.10 = (bf16[512,256]{0,1:T(8,128)(2,1)}, bf16[512,256]{0,1:T(8,128)(2,1)}, u32[]{:S(2)}, u32[]{:S(2)}) collective-permute-start(bf16[512,256]{0,1:T(8,128)(2,1)} %fusion.15), channel_id=1, source_target_pairs={{0,24},{4,28},{1,25},{5,29},{2,26},{6,30},{3,27},{7,31}} | collective-permute-start | bytes 786440 | tf_op jit(solution)/shard_map/ppermute | solution.py:16
  20.4 50.4 %collective-permute-start.11 = (bf16[512,256]{0,1:T(8,128)(2,1)}, bf16[512,256]{0,1:T(8,128)(2,1)}, u32[]{:S(2)}, u32[]{:S(2)}) collective-permute-start(bf16[512,256]{0,1:T(8,128)(2,1)} %fusion.15), channel_id=1, source_target_pairs={{0,20},{4,24},{8,28},{1,21},{5,25},{9,29},{2,22},{6,26},{10,30},{3... | collective-permute-start | bytes 786440 | tf_op jit(solution)/shard_map/ppermute | solution.py:16
  26.9 45.9 %collective-permute-start = (bf16[512,256]{1,0:T(8,128)(2,1)}, bf16[512,256]{1,0:T(8,128)(2,1)}, u32[]{:S(2)}, u32[]{:S(2)}) collective-permute-start(bf16[512,256]{1,0:T(8,128)(2,1)} %convolution_convert_fusion), channel_id=1, source_target_pairs={} | collective-permute-start | bytes 786440 | tf_op jit(solution)/shard_map/ppermute | solution.py:16
  36.8 3.1 %copy-start.4 = (f32[512,128]{1,0:T(8,128)S(1)}, f32[512,128]{1,0:T(8,128)}, u32[]{:S(2)}) copy-start(f32[512,128]{1,0:T(8,128)} %copy-done.3) | copy-start | bytes 786436
  39.8 1.7 copy-start.11
  41.5 31.3 %copy-start.8 = (bf16[512,2,2,128]{3,0,2,1:T(8,128)(2,1)}, bf16[512,2,2,128]{3,0,2,1:T(8,128)(2,1)S(1)}, u32[]{:S(2)}) copy-start(bf16[512,2,2,128]{3,0,2,1:T(8,128)(2,1)S(1)} %fusion.14) | copy-start | bytes 1572868
  65.0 10.1 %collective-permute-start.1 = (bf16[512,256]{1,0:T(8,128)(2,1)}, bf16[512,256]{1,0:T(8,128)(2,1)S(1)}, u32[]{:S(2)}, u32[]{:S(2)}) collective-permute-start(bf16[512,256]{1,0:T(8,128)(2,1)} %convolution_convert_fusion), channel_id=1, source_target_pairs={{0,28},{1,29},{2,30},{3,31}} | collective-permute-start | bytes 786440 | tf_op jit(solution)/shard_map/ppermute | solution.py:16
  68.2 22.3 %collective-permute-start.12 = (bf16[512,256]{0,1:T(8,128)(2,1)}, bf16[512,256]{0,1:T(8,128)(2,1)S(1)}, u32[]{:S(2)}, u32[]{:S(2)}) collective-permute-start(bf16[512,256]{0,1:T(8,128)(2,1)} %fusion.15), channel_id=1, source_target_pairs={{0,16},{4,20},{8,24},{12,28},{1,17},{5,21},{9,25},{13,29},{2,18},{... | collective-permute-start | bytes 786440 | tf_op jit(solution)/shard_map/ppermute | solution.py:16
  69.5 45.0 %collective-permute-start.13 = (bf16[512,256]{0,1:T(8,128)(2,1)}, bf16[512,256]{0,1:T(8,128)(2,1)S(1)}, u32[]{:S(2)}, u32[]{:S(2)}) collective-permute-start(bf16[512,256]{0,1:T(8,128)(2,1)} %fusion.15), channel_id=1, source_target_pairs={{0,12},{4,16},{8,20},{12,24},{16,28},{1,13},{5,17},{9,21},{13,25},... | collective-permute-start | bytes 786440 | tf_op jit(solution)/shard_map/ppermute | solution.py:16
  70.8 45.7 %collective-permute-start.2 = (bf16[512,256]{1,0:T(8,128)(2,1)}, bf16[512,256]{1,0:T(8,128)(2,1)S(1)}, u32[]{:S(2)}, u32[]{:S(2)}) collective-permute-start(bf16[512,256]{1,0:T(8,128)(2,1)} %convolution_convert_fusion), channel_id=1, source_target_pairs={{0,24},{4,28},{1,25},{5,29},{2,26},{6,30},{3,27},{7,31}} | collective-permute-start | bytes 786440 | tf_op jit(solution)/shard_map/ppermute | solution.py:16
  72.8 45.0 %collective-permute-start.3 = (bf16[512,256]{1,0:T(8,128)(2,1)}, bf16[512,256]{1,0:T(8,128)(2,1)S(1)}, u32[]{:S(2)}, u32[]{:S(2)}) collective-permute-start(bf16[512,256]{1,0:T(8,128)(2,1)} %convolution_convert_fusion), channel_id=1, source_target_pairs={{0,20},{4,24},{8,28},{1,21},{5,25},{9,29},{2,22},{6,26},{10,30},{3... | collective-permute-start | bytes 786440 | tf_op jit(solution)/shard_map/ppermute | solution.py:16
  75.1 47.6 %collective-permute-start.4 = (bf16[512,256]{1,0:T(8,128)(2,1)}, bf16[512,256]{1,0:T(8,128)(2,1)S(1)}, u32[]{:S(2)}, u32[]{:S(2)}) collective-permute-start(bf16[512,256]{1,0:T(8,128)(2,1)} %convolution_convert_fusion), channel_id=1, source_target_pairs={{0,16},{4,20},{8,24},{12,28},{1,17},{5,21},{9,25},{13,29},{2,18},{... | collective-permute-start | bytes 786440 | tf_op jit(solution)/shard_map/ppermute | solution.py:16
  90.5 40.4 %collective-permute-start.14 = (bf16[512,256]{0,1:T(8,128)(2,1)}, bf16[512,256]{0,1:T(8,128)(2,1)}, u32[]{:S(2)}, u32[]{:S(2)}) collective-permute-start(bf16[512,256]{0,1:T(8,128)(2,1)} %fusion.15), channel_id=1, source_target_pairs={{0,8},{4,12},{8,16},{12,20},{16,24},{20,28},{1,9},{5,13},{9,17},{1... | collective-permute-start | bytes 786440 | tf_op jit(solution)/shard_map/ppermute | solution.py:16
  114.6 10.3 %copy-start.10 = (bf16[512,256]{0,1:T(8,128)(2,1)}, bf16[512,256]{0,1:T(8,128)(2,1)S(1)}, u32[]{:S(2)}) copy-start(bf16[512,256]{0,1:T(8,128)(2,1)S(1)} %collective-permute-done.13) | copy-start | bytes 786436
  114.6 18.1 %collective-permute-start.15 = (bf16[512,256]{0,1:T(8,128)(2,1)}, bf16[512,256]{0,1:T(8,128)(2,1)}, u32[]{:S(2)}, u32[]{:S(2)}) collective-permute-start(bf16[512,256]{0,1:T(8,128)(2,1)} %fusion.15), channel_id=1, source_target_pairs={{0,4},{4,8},{8,12},{12,16},{16,20},{20,24},{24,28},{1,5},{5,9},{9,... | collective-permute-start | bytes 786440 | tf_op jit(solution)/shard_map/ppermute | solution.py:16
  116.5 26.4 %collective-permute-start.5 = (bf16[512,256]{1,0:T(8,128)(2,1)}, bf16[512,256]{1,0:T(8,128)(2,1)}, u32[]{:S(2)}, u32[]{:S(2)}) collective-permute-start(bf16[512,256]{1,0:T(8,128)(2,1)} %convolution_convert_fusion), channel_id=1, source_target_pairs={{0,12},{4,16},{8,20},{12,24},{16,28},{1,13},{5,17},{9,21},{13,25},... | collective-permute-start | bytes 786440 | tf_op jit(solution)/shard_map/ppermute | solution.py:16
  117.8 26.0 %collective-permute-start.6 = (bf16[512,256]{1,0:T(8,128)(2,1)}, bf16[512,256]{1,0:T(8,128)(2,1)}, u32[]{:S(2)}, u32[]{:S(2)}) collective-permute-start(bf16[512,256]{1,0:T(8,128)(2,1)} %convolution_convert_fusion), channel_id=1, source_target_pairs={{0,8},{4,12},{8,16},{12,20},{16,24},{20,28},{1,9},{5,13},{9,17},{1... | collective-permute-start | bytes 786440 | tf_op jit(solution)/shard_map/ppermute | solution.py:16
  122.7 25.6 %collective-permute-start.7 = (bf16[512,256]{1,0:T(8,128)(2,1)}, bf16[512,256]{1,0:T(8,128)(2,1)}, u32[]{:S(2)}, u32[]{:S(2)}) collective-permute-start(bf16[512,256]{1,0:T(8,128)(2,1)} %convolution_convert_fusion), channel_id=1, source_target_pairs={{0,4},{4,8},{8,12},{12,16},{16,20},{20,24},{24,28},{1,5},{5,9},{9,... | collective-permute-start | bytes 786440 | tf_op jit(solution)/shard_map/ppermute | solution.py:16
  152.8 9.8 %copy-start.6 = (pred[512,4608]{0,1:T(8,128)(4,1)S(1)}, pred[512,4608]{0,1:T(8,128)(4,1)}, u32[]{:S(2)}) copy-start(pred[512,4608]{0,1:T(8,128)(4,1)} %fusion.3) | copy-start | bytes 7077892
  152.8 9.8 %copy-start.9 = (bf16[512,2,2,128]{3,0,2,1:T(8,128)(2,1)S(1)}, bf16[512,2,2,128]{3,0,2,1:T(8,128)(2,1)}, u32[]{:S(2)}) copy-start(bf16[512,2,2,128]{3,0,2,1:T(8,128)(2,1)} %copy-done.8) | copy-start | bytes 1572868
  215.7 84.2 %copy-start.12 = (f32[1152]{0:T(1024)S(1)}, f32[1152]{0:T(1024)}, u32[]{:S(2)}) copy-start(f32[1152]{0:T(1024)} %param.13) | copy-start | bytes 13828
  299.9 3.9 %copy-start.1 = (bf16[4608,256]{1,0:T(8,128)(2,1)S(1)}, bf16[4608,256]{1,0:T(8,128)(2,1)}, u32[]{:S(2)}) copy-start(bf16[4608,256]{1,0:T(8,128)(2,1)} %param.10) | copy-start | bytes 7077892
Sparse Core Ops, SparseCore 0:
  208.6 83.0 reduce-scatter.1
where the time goes:
time: 314 us; the launch traced here: 311 us
  waiting for transfers between devices  128 us (41%)
  matrix products  60 us (19%)
  local copies, waits for them, and re-layouts  34.1 us (11%)
  other arithmetic  28.8 us (9%)
  blocking collectives  23 us (7%)
  starting transfers between devices  21.8 us (7%)
  between operations  14.6 us (5%)
    reduce_scatter x1, waiting for transfers between devices, on_device(): lax.psum_scatter(partial_rows, 'tp', scatter_dimension=1, tiled=True)  76 us
    ppermute x16, waiting for transfers between devices, shifted(): return lax.ppermute(x, axis, pairs)  52.4 us
    ppermute x16, starting transfers between devices, shifted(): return lax.ppermute(x, axis, pairs)  21.8 us
    dot_general x1, matrix products, one_block(): jnp.einsum('kgql,lkd->qkgd', weight.astype(jnp.bfloat16), value_block, pr...  19.5 us
    psum x1, blocking collectives, spread(): return lax.psum(kept, axis)  17.3 us
    dot_general x1, matrix products, one_block(): jnp.einsum('qkgd,lkd->kgql', query, key_block, preferred_element_type=jnp...  17.2 us
    unnamed x52, local copies, waits for them, and re-layouts  14.8 us
    concatenate x10, local copies, waits for them, and re-layouts, on_device(): keys_all = jnp.concatenate([piece[0] for piece in pieces] + [keys], axis=0)  12.6 us
  transfers between devices with their start and end apart: 17, of which 6 were waited for; matrix products, arithmetic and copies ran while one was open for 15% of the time, Pallas kernels for 0%

commit v1 on v0

--- a/solution.py
+++ b/solution.py
@@ -1,6 +1,10 @@
+import functools
+
 import jax
 import jax.numpy as jnp
 from jax import lax
+from jax.experimental import pallas as pl
+from jax.experimental.pallas import tpu as pltpu
 from jax.sharding import PartitionSpec as P
 
 D = 4608
@@ -132,9 +136,418 @@
     return (layer_out, sink_share)
 
 
+MESH = pl.DeviceIdType.MESH
+LOG2E = 1.4426950408889634
+
+
+def expo_of(query, keys):
+    scores = lax.dot_general(
+        query, keys, (((1,), (1,)), ((), ())), preferred_element_type=jnp.float32
+    )
+    return jnp.exp2((50.0 * LOG2E) * jnp.tanh(scores * (1.0 / 600.0)))
+
+
+def fused_kernel(
+    n,
+    hid_hbm,
+    wq_hbm,
+    wk_hbm,
+    wv_hbm,
+    wo_hbm,
+    gain_ref,
+    post_ref,
+    cos_ref,
+    sin_ref,
+    out_ref,
+    share_ref,
+    hid,
+    normed,
+    wq,
+    wk,
+    wv,
+    wo,
+    query,
+    kv,
+    acc,
+    sink_acc,
+    att,
+    proj,
+    stat,
+    hid_sem,
+    w_sem,
+    wo_own_sem,
+    wo_send,
+    wo_recv,
+    kv_send_z,
+    kv_send_y,
+    kv_recv,
+    att_send,
+    att_recv,
+    stat_send,
+    stat_recv,
+):
+    rows, width = hid.shape
+    cols = proj.shape[1]
+    q_width = query.shape[1]
+    kv_width = kv.shape[2] // 2
+    heads = q_width // HEAD
+    group = q_width // kv_width
+    levels = n // 2
+    c, t = lax.axis_index("ctx"), lax.axis_index("tp")
+    z, y = c // 2, lax.rem(c, 2)
+    mate = 2 * z + 1 - y
+    t_core = 2 * (t // 2) + 1 - lax.rem(t, 2)
+    t_far = lax.rem(t + 2, 4)
+    t_diag = lax.rem(t_core + 2, 4)
+    chunks = hid_sem.shape[0]
+    step_rows = rows // chunks
+
+    def hid_copy(i):
+        part = pl.ds(i * step_rows, step_rows)
+        return pltpu.make_async_copy(hid_hbm.at[part], hid.at[part], hid_sem.at[i])
+
+    for i in range(chunks):
+        hid_copy(i).start()
+    weights = [
+        pltpu.make_async_copy(a, b, w_sem.at[i])
+        for i, (a, b) in enumerate(((wk_hbm, wk), (wv_hbm, wv), (wq_hbm, wq)))
+    ]
+    for copy in weights:
+        copy.start()
+
+    barrier = pltpu.get_barrier_semaphore()
+    for other in (t_core, t_far, t_diag):
+        pl.semaphore_signal(barrier, inc=1, device_id=(c, other), device_id_type=MESH)
+    pl.semaphore_signal(barrier, inc=1, device_id=(mate, t), device_id_type=MESH)
+
+    @pl.when(z > 0)
+    def _():
+        pl.semaphore_signal(barrier, inc=1, device_id=(c - 2, t), device_id_type=MESH)
+
+    @pl.when(z < levels - 1)
+    def _():
+        pl.semaphore_signal(barrier, inc=1, device_id=(c + 2, t), device_id_type=MESH)
+
+    pl.semaphore_wait(barrier, 4 + jnp.minimum(z, 1) + jnp.minimum(levels - 1 - z, 1))
+
+    def wo_copy(i, other):
+        part = pl.ds(pl.multiple_of(other * cols, 128), cols)
+        return pltpu.make_async_remote_copy(
+            src_ref=wo_hbm.at[:, part],
+            dst_ref=wo.at[t],
+            send_sem=wo_send.at[i],
+            recv_sem=wo_recv.at[i],
+            device_id=(c, other),
+            device_id_type=MESH,
+        )
+
+    partners = (t_core, t_far, t_diag)
+    wo_copies = [wo_copy(i, other) for i, other in enumerate(partners)]
+    for i in (1, 2, 0):
+        wo_copies[i].start()
+    own_wo = pltpu.make_async_copy(
+        wo_hbm.at[:, pl.ds(pl.multiple_of(t * cols, 128), cols)], wo.at[t], wo_own_sem
+    )
+    own_wo.start()
+
+    norm_rows = 32
+    for i in range(chunks):
+        hid_copy(i).wait()
+
+        def norm_step(r, carry, i=i):
+            part = pl.ds(pl.multiple_of(i * step_rows + r * norm_rows, norm_rows), norm_rows)
+            x = hid[part, :].astype(jnp.float32)
+            scale = lax.rsqrt(jnp.sum(x * x, axis=-1, keepdims=True) * (1.0 / width) + 1e-06)
+            normed[part, :] = (x * scale * gain_ref[...]).astype(jnp.bfloat16)
+            return carry
+
+        lax.fori_loop(0, step_rows // norm_rows, norm_step, 0)
+
+    def rope(x):
+        return x * cos_ref[...] + pltpu.roll(x, HEAD // 2, 1) * sin_ref[...]
+
+    weights[0].wait()
+    keys = jnp.dot(normed[...], wk[...], preferred_element_type=jnp.float32)
+    for h in range(kv_width // HEAD):
+        cut = slice(h * HEAD, (h + 1) * HEAD)
+        kv[c, :, cut] = rope(keys[:, cut]).astype(jnp.bfloat16)
+    weights[1].wait()
+    values = jnp.dot(normed[...], wv[...], preferred_element_type=jnp.float32)
+    kv[c, :, kv_width:] = values.astype(jnp.bfloat16)
+
+    def up_copy(b):
+        return pltpu.make_async_remote_copy(
+            src_ref=kv.at[b],
+            dst_ref=kv.at[b],
+            send_sem=kv_send_z.at[b],
+            recv_sem=kv_recv.at[b],
+            device_id=(lax.rem(c + 2, n), t),
+            device_id_type=MESH,
+        )
+
+    def mate_copy(b):
+        return pltpu.make_async_remote_copy(
+            src_ref=kv.at[b],
+            dst_ref=kv.at[b],
+            send_sem=kv_send_y.at[b],
+            recv_sem=kv_recv.at[b],
+            device_id=(mate, t),
+            device_id_type=MESH,
+        )
+
+    @pl.when(z < levels - 1)
+    def _():
+        up_copy(c).start()
+
+    @pl.when(y == 0)
+    def _():
+        mate_copy(c).start()
+
+    weights[2].wait()
+
+    def query_step(i, carry):
+        part = pl.ds(pl.multiple_of(i * kv_width, kv_width), kv_width)
+        out = jnp.dot(normed[...], wq[:, part], preferred_element_type=jnp.float32)
+        for h in range(kv_width // HEAD):
+            cut = slice(h * HEAD, (h + 1) * HEAD)
+            here = pl.ds(pl.multiple_of(i * kv_width + h * HEAD, HEAD), HEAD)
+            query[:, here] = rope(out[:, cut]).astype(jnp.bfloat16)
+        return carry
+
+    lax.fori_loop(0, group, query_step, 0)
+
+    ones = jnp.ones((rows, HEAD), jnp.bfloat16)
+
+    def attend(b, own):
+        for h in range(heads):
+            k0 = (h // group) * HEAD
+            v0 = kv_width + k0
+            expo = expo_of(query[:, h * HEAD : (h + 1) * HEAD], kv[b, :, k0 : k0 + HEAD])
+            if own:
+                at = lax.broadcasted_iota(jnp.int32, (rows, rows), 0)
+                key_at = lax.broadcasted_iota(jnp.int32, (rows, rows), 1)
+                expo = jnp.where(key_at <= at, expo, 0.0)
+            more = jnp.concatenate([kv[b, :, v0 : v0 + HEAD], ones], axis=1)
+            part = jnp.dot(expo.astype(jnp.bfloat16), more, preferred_element_type=jnp.float32)
+            if own:
+                acc[h] = part
+            else:
+                acc[h] += part
+
+    attend(c, True)
+
+    def level_step(s, carry):
+        level = z - s
+
+        @pl.when(s > 0)
+        def _():
+            b = 2 * level + y
+            up_copy(b).wait_recv()
+
+            @pl.when(z < levels - 1)
+            def _():
+                up_copy(b).start()
+
+            mate_copy(b).start()
+            attend(b, False)
+
+        @pl.when((s > 0) | (y == 1))
+        def _():
+            b = 2 * level + 1 - y
+            mate_copy(b).wait_recv()
+            attend(b, False)
+
+        return carry
+
+    lax.fori_loop(0, z + 1, level_step, 0)
+
+    def att_copy(kind, h):
+        slot = t if kind < 2 else t_far
+        return pltpu.make_async_remote_copy(
+            src_ref=att.at[slot, h],
+            dst_ref=att.at[slot, h],
+            send_sem=att_send.at[kind, h],
+            recv_sem=att_recv.at[kind, h],
+            device_id=(c, t_far if kind == 0 else t_core),
+            device_id_type=MESH,
+        )
+
+    for h in range(heads):
+        att[t, h] = (acc[h, :, :HEAD] / acc[h, :, HEAD:]).astype(jnp.bfloat16)
+        att_copy(0, h).start()
+        att_copy(1, h).start()
+
+    lane = lax.broadcasted_iota(jnp.int32, (rows, HEAD), 1)
+    row = lax.broadcasted_iota(jnp.int32, (rows, HEAD), 0) + c * rows
+    sink_live = (lane < SINKS) & (lane <= row)
+    sinks = jnp.zeros((rows, HEAD), jnp.float32)
+    for h in range(heads):
+        k0 = (h // group) * HEAD
+        sinks += expo_of(query[:, h * HEAD : (h + 1) * HEAD], kv[0, :HEAD, k0 : k0 + HEAD])
+    sink_acc[...] = jnp.where(sink_live, sinks, 0.0)
+
+    tile = cols // 3
+
+    def add_slot(slot, first):
+        rows_of = jnp.concatenate([att[slot, h] for h in range(heads)], axis=1)
+        for i in range(3):
+            cut = slice(i * tile, (i + 1) * tile)
+            part = jnp.dot(rows_of, wo[slot, :, cut], preferred_element_type=jnp.float32)
+            if first:
+                proj[:, cut] = part
+            else:
+                proj[:, cut] += part
+
+    own_wo.wait()
+    add_slot(t, True)
+    wo_copies[0].wait_recv()
+    for h in range(heads):
+        att_copy(1, h).wait_recv()
+    add_slot(t_core, False)
+    for h in range(heads):
+        att_copy(0, h).wait_recv()
+        att_copy(2, h).start()
+    wo_copies[1].wait_recv()
+    add_slot(t_far, False)
+    wo_copies[2].wait_recv()
+    for h in range(heads):
+        att_copy(2, h).wait_recv()
+    add_slot(t_diag, False)
+
+    squares = jnp.sum(proj[...] * proj[...], axis=-1, keepdims=True)
+    sink_sum = jnp.sum(sink_acc[...], axis=-1, keepdims=True)
+    both = jnp.where(lane == 0, squares, sink_sum)
+    stat[t] = jnp.transpose(both)[:8, :]
+
+    def stat_copy(i, other):
+        return pltpu.make_async_remote_copy(
+            src_ref=stat.at[t],
+            dst_ref=stat.at[t],
+            send_sem=stat_send.at[i],
+            recv_sem=stat_recv.at[i],
+            device_id=(c, other),
+            device_id_type=MESH,
+        )
+
+    stats = [stat_copy(i, other) for i, other in enumerate(partners)]
+    for copy in stats:
+        copy.start()
+    for copy in stats:
+        copy.wait_recv()
+    total = stat[0] + stat[1] + stat[2] + stat[3]
+    share_ref[...] = jnp.log(total[1:2, :] / (4.0 * heads))
+    column = jnp.transpose(jnp.concatenate([total] * 16, axis=0))[:, :1]
+    scale = lax.rsqrt(column / width + 1e-06)
+    mine = hid[:, pl.ds(pl.multiple_of(t * cols, 128), cols)].astype(jnp.float32)
+    out_ref[...] = (mine + proj[...] * scale * post_ref[...]).astype(jnp.bfloat16)
+
+    @pl.when(z < levels - 1)
+    def _():
+        up_copy(c).wait_send()
+
+    @pl.when(y == 0)
+    def _():
+        mate_copy(c).wait_send()
+
+    def drain_step(s, carry):
+        b = 2 * (z - s) + y
+
+        @pl.when(z < levels - 1)
+        def _():
+            up_copy(b).wait_send()
+
+        mate_copy(b).wait_send()
+        return carry
+
+    lax.fori_loop(1, z + 1, drain_step, 0)
+    for copy in wo_copies + stats:
+        copy.wait_send()
+    for kind in range(3):
+        for h in range(heads):
+            att_copy(kind, h).wait_send()
+
+
+def fused_on_device(n, hidden_in, pre_gain, w_query, w_key, w_value, w_out, post_gain):
+    rows, width = hidden_in.shape
+    cols = post_gain.shape[0]
+    q_width, kv_width = w_query.shape[1], w_key.shape[1]
+    heads = q_width // HEAD
+    positions = lax.axis_index("ctx") * rows + jnp.arange(rows, dtype=jnp.int32)
+    cosine, sine = rope_tables(positions)
+    cosine, sine = cosine[:, 0, :], sine[:, 0, :]
+    sine = jnp.where(jnp.arange(HEAD)[None, :] < HEAD // 2, -sine, sine)
+    hbm, vmem = pl.BlockSpec(memory_space=pl.ANY), pl.BlockSpec(memory_space=pltpu.VMEM)
+    dma = pltpu.SemaphoreType.DMA
+    bf16, f32 = jnp.bfloat16, jnp.float32
+    layer_out, share = pl.pallas_call(
+        functools.partial(fused_kernel, n),
+        out_shape=(
+            jax.ShapeDtypeStruct((rows, cols), bf16),
+            jax.ShapeDtypeStruct((1, rows), f32),
+        ),
+        in_specs=[hbm] * 5 + [vmem] * 4,
+        out_specs=(vmem, vmem),
+        scratch_shapes=[
+            pltpu.VMEM((rows, width), bf16),
+            pltpu.VMEM((rows, width), bf16),
+            pltpu.VMEM((width, q_width), bf16),
+            pltpu.VMEM((width, kv_width), bf16),
+            pltpu.VMEM((width, kv_width), bf16),
+            pltpu.VMEM((4, q_width, cols), bf16),
+            pltpu.VMEM((rows, q_width), bf16),
+            pltpu.VMEM((n, rows, 2 * kv_width), bf16),
+            pltpu.VMEM((heads, rows, 2 * HEAD), f32),
+            pltpu.VMEM((rows, HEAD), f32),
+            pltpu.VMEM((4, heads, rows, HEAD), bf16),
+            pltpu.VMEM((rows, cols), f32),
+            pltpu.VMEM((4, 8, rows), f32),
+            dma((4,)),
+            dma((3,)),
+            dma,
+            dma((3,)),
+            dma((3,)),
+            dma((n,)),
+            dma((n,)),
+            dma((n,)),
+            dma((3, heads)),
+            dma((3, heads)),
+            dma((3,)),
+            dma((3,)),
+        ],
+        compiler_params=pltpu.CompilerParams(
+            collective_id=0, has_side_effects=True, vmem_limit_bytes=56 * 1024 * 1024
+        ),
+        cost_estimate=pl.CostEstimate(
+            flops=2 * rows * width * (q_width + 2 * kv_width)
+            + 4 * rows * n * rows * q_width
+            + 8 * rows * q_width * cols,
+            bytes_accessed=2 * width * (rows + 2 * q_width + 2 * kv_width),
+            transcendentals=2 * heads * rows * n * rows,
+        ),
+    )(
+        hidden_in,
+        w_query,
+        w_key,
+        w_value,
+        w_out,
+        pre_gain.reshape(1, width),
+        post_gain.reshape(1, cols),
+        cosine,
+        sine,
+    )
+    return layer_out, share.reshape(rows)
+
+
 def solution(mesh):
+    n, tp = mesh.shape["ctx"], mesh.shape["tp"]
+
+    def body(*args):
+        if n * args[0].shape[0] <= WINDOW and n % 2 == 0 and tp == 4:
+            return fused_on_device(n, *args)
+        return on_device(*args)
+
     return jax.shard_map(
-        on_device,
+        body,
         mesh=mesh,
         in_specs=(
             P("ctx", None),

time: 314 us -> 92.1 us (0.29); the launches traced: 311 us -> 91.9 us
  waiting for transfers between devices: 128 us -> 0 us
  Pallas kernels: 0 us -> 83.6 us
  matrix products: 60 us -> 0 us
  local copies, waits for them, and re-layouts: 34.1 us -> 5.6 us
  other arithmetic: 28.8 us -> 1.98 us
  blocking collectives: 23 us -> 0 us
  starting transfers between devices: 21.8 us -> 0 us
  between operations: 14.6 us -> 0.68 us
    pallas_call x0 -> x1, Pallas kernels: none -> 83.6 us  [fused_on_device(): pl.pallas_call(functools.partial(fused_kernel, n), out_shape=(jax.ShapeDt...]
    reduce_scatter x1 -> x0, waiting for transfers between devices: 76 us -> none  [on_device(): lax.psum_scatter(partial_rows, 'tp', scatter_dimension=1, tiled=True)]
    dot_general x8 -> x0, matrix products: 60 us -> none  [the longest x1 19.5 us: one_block(): jnp.einsum('kgql,lkd->qkgd', weight.astype(jnp.bfloat16), value_block, pr...]
    ppermute x16 -> x0, waiting for transfers between devices: 52.4 us -> none  [shifted(): return lax.ppermute(x, axis, pairs)]
    psum x2 -> x0, blocking collectives: 23 us -> none  [the longest x1 17.3 us: spread(): return lax.psum(kept, axis)]
    ppermute x16 -> x0, starting transfers between devices: 21.8 us -> none  [shifted(): return lax.ppermute(x, axis, pairs)]
    convert_element_type x4 -> x0, other arithmetic: 13.6 us -> none  [the longest x1 7.24 us: on_device(): inputs = hidden_in.astype(jnp.float32)]
    concatenate x11 -> x0, local copies, waits for them, and re-layouts: 13.5 us -> none  [the longest x10 12.6 us: on_device(): keys_all = jnp.concatenate([piece[0] for piece in pieces] + [keys], axis=0)]
  transfers between devices with their start and end apart: 17 -> 0, of which waited for: 6 -> 0; matrix products, arithmetic and copies ran while one was open for 15% -> 0% of each run, Pallas kernels for 0% -> 0%
where the time goes in v1:
time: 92.1 us; the launch traced here: 91.9 us
  Pallas kernels  83.6 us (91%)
  local copies, waits for them, and re-layouts  5.6 us (6%)
  other arithmetic  1.98 us (2%)
    pallas_call x1, Pallas kernels, fused_on_device(): pl.pallas_call(functools.partial(fused_kernel, n), out_shape=(jax.ShapeDt...  83.6 us
    unnamed x4, local copies, waits for them, and re-layouts  2.96 us

profile of v1, /device:TPU:25, one launch (start us, length us, event | category | flops | bytes accessed | tf_op | source)
XLA Modules:
  0.0 91.9 jit_solution(2015357669816477799)
XLA Ops:
  0.7 1.3 %reshape.31.post_ref = f32[1,1152]{1,0:T(1,128)} reshape(f32[1152]{0:T(1024)} %param.13) | data formatting | bytes 9216 | tf_op jit(solution)/shard_map/reshape | solution.py:534
  2.0 1.3 %reshape.30.gain_ref = f32[1,4608]{1,0:T(1,128)} reshape(f32[4608]{0:T(1024)} %param.8) | data formatting | bytes 36864 | tf_op jit(solution)/shard_map/reshape | solution.py:533
  3.3 0.1 broadcast_multiply_fusion
  3.4 1.8 %negate_select_fusion = (f32[512,128]{1,0:T(8,128)}, f32[512,128]{1,0:T(8,128)}) fusion(f32[512,64]{1,0:T(8,128)S(1)} %broadcast_multiply_fusion, pred[128]{0:T(512)(128)(4,1)S(1)} %iota_compare_fusion), kind=kLoop, calls=%fused_computation | loop fusion | flops 196608 | bytes 655488 | tf_op jit(solution)/shard_map/jit(_where)/select_n | solution.py:478
  5.3 83.6 %shard_map.86 = (bf16[512,1152]{1,0:T(8,128)(2,1)}, f32[1,512]{1,0:T(1,128)}) custom-call(bf16[512,4608]{1,0:T(8,128)(2,1)} %hid_hbm.1, bf16[4608,512]{1,0:T(8,128)(2,1)} %wq_hbm.1, bf16[4608,256]{1,0:T(8,128)(2,1)} %wk_hbm.1, bf16[4608,256]{1,0:T(8,128)(2,1)} %wv_hbm.1, bf16[512,4608]{1,0:T(8,128)(2,1)} %wo_hbm.1, f32[1,4608]{1,0:T(1,128)} %reshape.30.gain_ref, ...), custom_call_target="tpu_custom_call" | custom-call | flops 11542724608 | bytes 18874368 | tf_op jit(solution)/shard_map/pallas_call | solution.py:482
  88.9 0.0 copy-start
  88.9 2.4 %copy.11 = bf16[512,1152]{1,0:T(8,128)(2,1)} copy(bf16[512,1152]{1,0:T(8,128)(2,1)} %get-tuple-element.10) | data formatting | bytes 2359296
  91.3 0.0 copy-done
  91.3 0.6 copy.12
  (3 shorter events, 0.0 us)
Async XLA Ops:
  88.9 2.4 %copy-start = (f32[1,512]{1,0:T(1,128)S(1)}, f32[1,512]{1,0:T(1,128)}, u32[]{:S(2)}) copy-start(f32[1,512]{1,0:T(1,128)} %get-tuple-element.5) | copy-start | bytes 6148

commit v2 on v1

--- a/solution.py
+++ b/solution.py
@@ -181,6 +181,13 @@
     kv_send_z,
     kv_send_y,
     kv_recv,
+    v_send,
+    v_recv,
+    tail_send,
+    tail_recv,
+    end_send,
+    down_send,
+    end_recv,
     att_send,
     att_recv,
     stat_send,
@@ -230,11 +237,15 @@
 
     pl.semaphore_wait(barrier, 4 + jnp.minimum(z, 1) + jnp.minimum(levels - 1 - z, 1))
 
+    end = q_width // 8
+    bulk = q_width - 2 * end
+
     def wo_copy(i, other):
         part = pl.ds(pl.multiple_of(other * cols, 128), cols)
-        return pltpu.make_async_remote_copy(
-            src_ref=wo_hbm.at[:, part],
-            dst_ref=wo.at[t],
+        span = pl.ds(0, q_width if i == 0 else bulk)
+        return pltpu.make_async_remote_copy(
+            src_ref=wo_hbm.at[span, part],
+            dst_ref=wo.at[t, span],
             send_sem=wo_send.at[i],
             recv_sem=wo_recv.at[i],
             device_id=(c, other),
@@ -243,6 +254,34 @@
 
     partners = (t_core, t_far, t_diag)
     wo_copies = [wo_copy(i, other) for i, other in enumerate(partners)]
+
+    def tail_copy(i, other):
+        part = pl.ds(pl.multiple_of(other * cols, 128), cols)
+        span = pl.ds(pl.multiple_of(bulk + end * (1 - jnp.minimum(z, 1)), 16), end)
+        return pltpu.make_async_remote_copy(
+            src_ref=wo_hbm.at[span, part],
+            dst_ref=wo.at[t, span],
+            send_sem=tail_send.at[i],
+            recv_sem=tail_recv.at[i],
+            device_id=(c, other),
+            device_id_type=MESH,
+        )
+
+    def end_copy(i, up):
+        slot = (t_far, t_diag)[i]
+        span = pl.ds(bulk + end if up else bulk, end)
+        return pltpu.make_async_remote_copy(
+            src_ref=wo.at[slot, span],
+            dst_ref=wo.at[slot, span],
+            send_sem=end_send.at[i] if up else down_send.at[i],
+            recv_sem=end_recv.at[i],
+            device_id=(lax.rem(c + 2 if up else c + n - 2, n), t),
+            device_id_type=MESH,
+        )
+
+    tails = [tail_copy(0, t_far), tail_copy(1, t_diag)]
+    for copy in tails:
+        copy.start()
     for i in (1, 2, 0):
         wo_copies[i].start()
     own_wo = pltpu.make_async_copy(
@@ -258,7 +297,7 @@
             part = pl.ds(pl.multiple_of(i * step_rows + r * norm_rows, norm_rows), norm_rows)
             x = hid[part, :].astype(jnp.float32)
             scale = lax.rsqrt(jnp.sum(x * x, axis=-1, keepdims=True) * (1.0 / width) + 1e-06)
-            normed[part, :] = (x * scale * gain_ref[...]).astype(jnp.bfloat16)
+            normed[part, :] = (x * scale * gain_ref[...].reshape(1, width)).astype(jnp.bfloat16)
             return carry
 
         lax.fori_loop(0, step_rows // norm_rows, norm_step, 0)
@@ -292,6 +331,28 @@
             send_sem=kv_send_y.at[b],
             recv_sem=kv_recv.at[b],
             device_id=(mate, t),
+            device_id_type=MESH,
+        )
+
+    def mate_keys(b):
+        part = pl.ds(0, kv_width)
+        return pltpu.make_async_remote_copy(
+            src_ref=kv.at[b, :, part],
+            dst_ref=kv.at[b, :, part],
+            send_sem=kv_send_y.at[b],
+            recv_sem=kv_recv.at[b],
+            device_id=(mate, t),
+            device_id_type=MESH,
+        )
+
+    def up_values(b):
+        part = pl.ds(kv_width, kv_width)
+        return pltpu.make_async_remote_copy(
+            src_ref=kv.at[b, :, part],
+            dst_ref=kv.at[b, :, part],
+            send_sem=v_send,
+            recv_sem=v_recv,
+            device_id=(lax.rem(c + 2, n), t),
             device_id_type=MESH,
         )
 
@@ -348,13 +409,36 @@
             def _():
                 up_copy(b).start()
 
-            mate_copy(b).start()
+            half = (s == 1) & (y == 0)
+
+            @pl.when(half)
+            def _():
+                mate_keys(b).start()
+
+            @pl.when(jnp.logical_not(half))
+            def _():
+                mate_copy(b).start()
+
             attend(b, False)
 
         @pl.when((s > 0) | (y == 1))
         def _():
             b = 2 * level + 1 - y
-            mate_copy(b).wait_recv()
+            half = (s == 1) & (y == 1)
+
+            @pl.when(half)
+            def _():
+                mate_keys(b).wait_recv()
+                up_values(b).wait_recv()
+
+            @pl.when(jnp.logical_not(half))
+            def _():
+                mate_copy(b).wait_recv()
+
+            @pl.when((s == 0) & (z < levels - 1))
+            def _():
+                up_values(b).start()
+
             attend(b, False)
 
         return carry
@@ -376,6 +460,24 @@
         att[t, h] = (acc[h, :, :HEAD] / acc[h, :, HEAD:]).astype(jnp.bfloat16)
         att_copy(0, h).start()
         att_copy(1, h).start()
+
+    for copy in tails:
+        copy.wait_recv()
+
+    @pl.when(z == 1)
+    def _():
+        end_copy(0, False).start()
+        end_copy(1, False).start()
+
+    @pl.when(z > 0)
+    def _():
+        end_copy(0, True).wait_recv()
+        end_copy(1, True).wait_recv()
+
+    @pl.when(z < levels - 1)
+    def _():
+        end_copy(0, True).start()
+        end_copy(1, True).start()
 
     lane = lax.broadcasted_iota(jnp.int32, (rows, HEAD), 1)
     row = lax.broadcasted_iota(jnp.int32, (rows, HEAD), 0) + c * rows
@@ -408,6 +510,12 @@
         att_copy(0, h).wait_recv()
         att_copy(2, h).start()
     wo_copies[1].wait_recv()
+
+    @pl.when(z == 0)
+    def _():
+        end_copy(0, False).wait_recv()
+        end_copy(1, False).wait_recv()
+
     add_slot(t_far, False)
     wo_copies[2].wait_recv()
     for h in range(heads):
@@ -439,11 +547,22 @@
     column = jnp.transpose(jnp.concatenate([total] * 16, axis=0))[:, :1]
     scale = lax.rsqrt(column / width + 1e-06)
     mine = hid[:, pl.ds(pl.multiple_of(t * cols, 128), cols)].astype(jnp.float32)
-    out_ref[...] = (mine + proj[...] * scale * post_ref[...]).astype(jnp.bfloat16)
+    out_ref[...] = (mine + proj[...] * scale * post_ref[...].reshape(1, cols)).astype(jnp.bfloat16)
 
     @pl.when(z < levels - 1)
     def _():
         up_copy(c).wait_send()
+        end_copy(0, True).wait_send()
+        end_copy(1, True).wait_send()
+
+    @pl.when((z < levels - 1) & (y == 1))
+    def _():
+        up_values(c - 1).wait_send()
+
+    @pl.when(z == 1)
+    def _():
+        end_copy(0, False).wait_send()
+        end_copy(1, False).wait_send()
 
     @pl.when(y == 0)
     def _():
@@ -456,11 +575,20 @@
         def _():
             up_copy(b).wait_send()
 
-        mate_copy(b).wait_send()
+        half = (s == 1) & (y == 0)
+
+        @pl.when(half)
+        def _():
+            mate_keys(b).wait_send()
+
+        @pl.when(jnp.logical_not(half))
+        def _():
+            mate_copy(b).wait_send()
+
         return carry
 
     lax.fori_loop(1, z + 1, drain_step, 0)
-    for copy in wo_copies + stats:
+    for copy in wo_copies + tails + stats:
         copy.wait_send()
     for kind in range(3):
         for h in range(heads):
@@ -509,6 +637,13 @@
             dma((n,)),
             dma((n,)),
             dma((n,)),
+            dma,
+            dma,
+            dma((2,)),
+            dma((2,)),
+            dma((2,)),
+            dma((2,)),
+            dma((2,)),
             dma((3, heads)),
             dma((3, heads)),
             dma((3,)),
@@ -530,8 +665,8 @@
         w_key,
         w_value,
         w_out,
-        pre_gain.reshape(1, width),
-        post_gain.reshape(1, cols),
+        pre_gain,
+        post_gain,
         cosine,
         sine,
     )
@@ -542,7 +677,7 @@
     n, tp = mesh.shape["ctx"], mesh.shape["tp"]
 
     def body(*args):
-        if n * args[0].shape[0] <= WINDOW and n % 2 == 0 and tp == 4:
+        if n * args[0].shape[0] <= WINDOW and n % 2 == 0 and n >= 4 and tp == 4:
             return fused_on_device(n, *args)
         return on_device(*args)
 

time: 92.1 us -> 91 us (0.988)
  local copies, waits for them, and re-layouts: 5.6 us -> 2.96 us
  Pallas kernels: 83.6 us -> 84.6 us
    reshape x2 -> x0, local copies, waits for them, and re-layouts: 2.64 us -> none  [the longest x1 1.35 us: fused_on_device(): pre_gain.reshape(1, width)]
    pallas_call x1, Pallas kernels: 83.6 us -> 84.6 us  [fused_on_device(): pl.pallas_call(functools.partial(fused_kernel, n), out_shape=(jax.ShapeDt...]
where the time goes in v2:
time: 91 us; the launch traced here: 90.2 us
  Pallas kernels  84.6 us (93%)
  local copies, waits for them, and re-layouts  2.96 us (3%)
  other arithmetic  1.99 us (2%)
    pallas_call x1, Pallas kernels, fused_on_device(): pl.pallas_call(functools.partial(fused_kernel, n), out_shape=(jax.ShapeDt...  84.6 us
    unnamed x4, local copies, waits for them, and re-layouts  2.96 us
    select_n x1, other arithmetic, fused_on_device(): sine = jnp.where(jnp.arange(HEAD)[None, :] < HEAD // 2, -sine, sine)  1.84 us

profile of v2, /device:TPU:25, one launch (start us, length us, event | category | flops | bytes accessed | tf_op | source)
XLA Modules:
  0.0 90.2 jit_solution(5102973060076107235)
XLA Ops:
  0.7 0.1 broadcast_multiply_fusion
  0.8 1.8 %negate_select_fusion = (f32[512,128]{1,0:T(8,128)}, f32[512,128]{1,0:T(8,128)}) fusion(f32[512,64]{1,0:T(8,128)S(1)} %broadcast_multiply_fusion, pred[128]{0:T(512)(128)(4,1)S(1)} %iota_compare_fusion), kind=kLoop, calls=%fused_computation | loop fusion | flops 196608 | bytes 655488 | tf_op jit(solution)/shard_map/jit(_where)/select_n | solution.py:606
  2.6 84.6 %shard_map.86 = (bf16[512,1152]{1,0:T(8,128)(2,1)}, f32[1,512]{1,0:T(1,128)}) custom-call(bf16[512,4608]{1,0:T(8,128)(2,1)} %hid_hbm.1, bf16[4608,512]{1,0:T(8,128)(2,1)} %wq_hbm.1, bf16[4608,256]{1,0:T(8,128)(2,1)} %wk_hbm.1, bf16[4608,256]{1,0:T(8,128)(2,1)} %wv_hbm.1, bf16[512,4608]{1,0:T(8,128)(2,1)} %wo_hbm.1, f32[4608]{0:T(1024)} %gain_ref.1, ...), custom_call_target="tpu_custom_call" | custom-call | flops 11542724608 | bytes 18874368 | tf_op jit(solution)/shard_map/pallas_call | solution.py:610
  87.2 0.0 copy-start
  87.3 2.4 %copy.11 = bf16[512,1152]{1,0:T(8,128)(2,1)} copy(bf16[512,1152]{1,0:T(8,128)(2,1)} %get-tuple-element.10) | data formatting | bytes 2359296
  89.6 0.0 copy-done
  89.6 0.6 copy.12
  (3 shorter events, 0.0 us)
Async XLA Ops:
  87.2 2.4 %copy-start = (f32[1,512]{1,0:T(1,128)S(1)}, f32[1,512]{1,0:T(1,128)}, u32[]{:S(2)}) copy-start(f32[1,512]{1,0:T(1,128)} %get-tuple-element.5) | copy-start | bytes 6148

commit v3 on v2

--- a/solution.py
+++ b/solution.py
@@ -181,8 +181,6 @@
     kv_send_z,
     kv_send_y,
     kv_recv,
-    v_send,
-    v_recv,
     tail_send,
     tail_recv,
     end_send,
@@ -334,28 +332,6 @@
             device_id_type=MESH,
         )
 
-    def mate_keys(b):
-        part = pl.ds(0, kv_width)
-        return pltpu.make_async_remote_copy(
-            src_ref=kv.at[b, :, part],
-            dst_ref=kv.at[b, :, part],
-            send_sem=kv_send_y.at[b],
-            recv_sem=kv_recv.at[b],
-            device_id=(mate, t),
-            device_id_type=MESH,
-        )
-
-    def up_values(b):
-        part = pl.ds(kv_width, kv_width)
-        return pltpu.make_async_remote_copy(
-            src_ref=kv.at[b, :, part],
-            dst_ref=kv.at[b, :, part],
-            send_sem=v_send,
-            recv_sem=v_recv,
-            device_id=(lax.rem(c + 2, n), t),
-            device_id_type=MESH,
-        )
-
     @pl.when(z < levels - 1)
     def _():
         up_copy(c).start()
@@ -409,36 +385,13 @@
             def _():
                 up_copy(b).start()
 
-            half = (s == 1) & (y == 0)
-
-            @pl.when(half)
-            def _():
-                mate_keys(b).start()
-
-            @pl.when(jnp.logical_not(half))
-            def _():
-                mate_copy(b).start()
-
+            mate_copy(b).start()
             attend(b, False)
 
         @pl.when((s > 0) | (y == 1))
         def _():
             b = 2 * level + 1 - y
-            half = (s == 1) & (y == 1)
-
-            @pl.when(half)
-            def _():
-                mate_keys(b).wait_recv()
-                up_values(b).wait_recv()
-
-            @pl.when(jnp.logical_not(half))
-            def _():
-                mate_copy(b).wait_recv()
-
-            @pl.when((s == 0) & (z < levels - 1))
-            def _():
-                up_values(b).start()
-
+            mate_copy(b).wait_recv()
             attend(b, False)
 
         return carry
@@ -555,10 +508,6 @@
         end_copy(0, True).wait_send()
         end_copy(1, True).wait_send()
 
-    @pl.when((z < levels - 1) & (y == 1))
-    def _():
-        up_values(c - 1).wait_send()
-
     @pl.when(z == 1)
     def _():
         end_copy(0, False).wait_send()
@@ -575,16 +524,7 @@
         def _():
             up_copy(b).wait_send()
 
-        half = (s == 1) & (y == 0)
-
-        @pl.when(half)
-        def _():
-            mate_keys(b).wait_send()
-
-        @pl.when(jnp.logical_not(half))
-        def _():
-            mate_copy(b).wait_send()
-
+        mate_copy(b).wait_send()
         return carry
 
     lax.fori_loop(1, z + 1, drain_step, 0)
@@ -637,8 +577,6 @@
             dma((n,)),
             dma((n,)),
             dma((n,)),
-            dma,
-            dma,
             dma((2,)),
             dma((2,)),
             dma((2,)),

time: 91 us -> 89.5 us (0.984)
  no operation moved by 1% of the time
where the time goes in v3:
time: 89.5 us; the launch traced here: 89.3 us
  Pallas kernels  83.7 us (94%)
  local copies, waits for them, and re-layouts  2.96 us (3%)
  other arithmetic  1.99 us (2%)
    pallas_call x1, Pallas kernels, fused_on_device(): pl.pallas_call(functools.partial(fused_kernel, n), out_shape=(jax.ShapeDt...  83.7 us
    unnamed x4, local copies, waits for them, and re-layouts  2.96 us
    select_n x1, other arithmetic, fused_on_device(): sine = jnp.where(jnp.arange(HEAD)[None, :] < HEAD // 2, -sine, sine)  1.84 us

profile of v3, /device:TPU:25, one launch (start us, length us, event | category | flops | bytes accessed | tf_op | source)
XLA Modules:
  0.0 89.3 jit_solution(10867704267696755061)
XLA Ops:
  0.7 0.1 broadcast_multiply_fusion
  0.8 1.8 %negate_select_fusion = (f32[512,128]{1,0:T(8,128)}, f32[512,128]{1,0:T(8,128)}) fusion(f32[512,64]{1,0:T(8,128)S(1)} %broadcast_multiply_fusion, pred[128]{0:T(512)(128)(4,1)S(1)} %iota_compare_fusion), kind=kLoop, calls=%fused_computation | loop fusion | flops 196608 | bytes 655488 | tf_op jit(solution)/shard_map/jit(_where)/select_n | solution.py:546
  2.6 83.7 %shard_map.86 = (bf16[512,1152]{1,0:T(8,128)(2,1)}, f32[1,512]{1,0:T(1,128)}) custom-call(bf16[512,4608]{1,0:T(8,128)(2,1)} %hid_hbm.1, bf16[4608,512]{1,0:T(8,128)(2,1)} %wq_hbm.1, bf16[4608,256]{1,0:T(8,128)(2,1)} %wk_hbm.1, bf16[4608,256]{1,0:T(8,128)(2,1)} %wv_hbm.1, bf16[512,4608]{1,0:T(8,128)(2,1)} %wo_hbm.1, f32[4608]{0:T(1024)} %gain_ref.1, ...), custom_call_target="tpu_custom_call" | custom-call | flops 11542724608 | bytes 18874368 | tf_op jit(solution)/shard_map/pallas_call | solution.py:550
  86.4 0.0 copy-start
  86.4 2.4 %copy.11 = bf16[512,1152]{1,0:T(8,128)(2,1)} copy(bf16[512,1152]{1,0:T(8,128)(2,1)} %get-tuple-element.10) | data formatting | bytes 2359296
  88.7 0.0 copy-done
  88.7 0.6 copy.12
  (3 shorter events, 0.0 us)
Async XLA Ops:
  86.4 2.4 %copy-start = (f32[1,512]{1,0:T(1,128)S(1)}, f32[1,512]{1,0:T(1,128)}, u32[]{:S(2)}) copy-start(f32[1,512]{1,0:T(1,128)} %get-tuple-element.5) | copy-start | bytes 6148
